TPU v7x, 32 devices: a whole 2x2x4 slice. The times are simulated.
32 devices in a mesh: lat: 4 (over y, x), lon: 8 (over z, core).
Axes of the slice: x: 2, y: 2, z: 4, core: 2. Of those that a mesh axis runs over, the one named last changes fastest.
Arguments:
- background: bfloat16 [64, 256, 512], P('lat', 'lon'), may hold values from -6 to 6
- observations: bfloat16 [32768, 256], P(('lat', 'lon')), may hold values from -6 to 6
- destination: int32 [32768, 1], P(('lat', 'lon')), may hold values from 0 to 31; in each aligned block of 1024 rows (0 to 1023, 1024 to 2047, ...) at most 64 rows name the same one
- footprint: int32 [32768, 4], P(('lat', 'lon')), may hold values from 0 to 511, as said below
- weights: bfloat16 [32768, 4], P(('lat', 'lon')), may hold values from 0.099609375 to 1
- obs_proj: bfloat16 [256, 512], replicated, may hold values from -0.375 to 0.375
- depth_w: float32 [4, 7, 7, 512], replicated, may hold values from -1.5 to 1.5
- point_w: bfloat16 [4, 512, 512], replicated, may hold values from -0.25 to 0.25
- gains: float32 [4, 512], replicated, may hold values from 0.5 to 2
Outputs:
- encoded: bfloat16 [64, 256, 512], P('lat', 'lon')
Inputs may be any that keep to these rules, and one draw needn't show every extreme that they name: `destination`: each device's 1024 rows name one tile at most 64 times. footprint[i, k] = (s_i + k * 33) mod 512 for a start cell s_i, so the 4 cells of one observation are distinct.
All inputs are finite; a program needn't handle non-finite values.
Results may differ from a plain program's by a relative error of at most 0.0085.
Values may be sent and summed in bfloat16 or wider, within the bound.
No kernel may reach another device: no remote copies, remote signals or barrier semaphores. Data moves between devices by JAX's collectives and lax.ppermute only.
A program may use at most 64 MiB of HBM per device.

v0:
```python
import functools

import jax
import jax.numpy as jnp
from jax import lax
from jax.experimental import pallas as pl
from jax.experimental.pallas import tpu as pltpu
from jax.sharding import PartitionSpec as P

LANES = 128
META = 8
TAPS = 7
HALO = 3
SHIFT = 2 * HALO
EDGE = 8
TILE = 16
MICROSECOND = 1150000000
WORK = 40000
VMEM_LIMIT = 24 * 1024 * 1024
PACK_LIMIT = 58 * 1024 * 1024
BF16 = jnp.bfloat16
F32 = jnp.float32


def place(cap, first, dest, rank, meta, obs, send_ref):
    members, depth, _ = send_ref.shape
    obs_rows = obs.shape[0]
    per = LANES // cap
    slot = lax.broadcasted_iota(jnp.int32, (cap, obs_rows), 0)
    ranked = jnp.where(slot == rank, 1.0, 0.0).astype(BF16).reshape(cap // TILE, TILE, obs_rows)
    lane = lax.broadcasted_iota(jnp.int32, (META, LANES), 1)
    count = min(512, members * cap) // cap
    for start in range(0, members, count):
        parts = []
        for d in range(start, start + count):
            mine = jnp.where(dest == first + d, 1.0, 0.0)
            mine = jnp.broadcast_to(mine, (TILE, obs_rows)).astype(BF16)
            parts.append((ranked * mine[None]).reshape(cap, obs_rows))
        chosen = jnp.concatenate(parts, axis=0)
        feats = jnp.dot(chosen, obs, preferred_element_type=F32).astype(BF16)
        placed = lax.dot_general(
            meta, chosen, (((1,), (1,)), ((), ())), preferred_element_type=F32
        )
        for half in range(feats.shape[1] // LANES):
            piece = feats[:, half * LANES : (half + 1) * LANES].reshape(count, cap, LANES)
            send_ref[start : start + count, half * cap : (half + 1) * cap, :] = piece
        for chunk in range(count // per):
            values = placed[:, chunk * LANES : (chunk + 1) * LANES]
            turned = [values] + [pltpu.roll(values, k * cap, 1) for k in range(1, per)]
            for own in range(per):
                wide = turned[0]
                for group in range(per):
                    wide = jnp.where(lane // cap == group, turned[(group - own) % per], wide)
                send_ref[start + chunk * per + own, depth - META :, :] = wide.astype(BF16)


def far_kernel(
    cap,
    cols,
    lon,
    dest_hbm,
    foot_hbm,
    weights_hbm,
    obs_hbm,
    send_ref,
    order_ref,
    meta_ref,
    dest_ref,
    foot_ref,
    weights_ref,
    obs_ref,
    sems,
):
    copies = [
        pltpu.make_async_copy(source, target, sems.at[k])
        for k, (source, target) in enumerate(
            (
                (dest_hbm, dest_ref),
                (obs_hbm, obs_ref),
                (foot_hbm, foot_ref),
                (weights_hbm, weights_ref),
            )
        )
    ]
    for copy in copies:
        copy.start()
    members = send_ref.shape[0]
    obs_rows = obs_ref.shape[0]
    half = lon // 2
    upper = lax.broadcasted_iota(jnp.int32, (LANES, LANES), 0) <= lax.broadcasted_iota(
        jnp.int32, (LANES, LANES), 1
    )
    upper = jnp.where(upper, 1.0, 0.0).astype(BF16)
    ids = lax.broadcasted_iota(jnp.int32, (2 * members, obs_rows), 0)
    skip = lax.div(lax.axis_index("lon"), half) * half
    copies[0].wait()
    target = dest_ref[...]
    across = lax.rem(target, lon) - skip
    across = jnp.where(across < 0, across + lon, across)
    dest = lax.div(target, lon) * half + across
    dest = jnp.where(across >= half, dest + (members - half), dest)
    member = jnp.where(ids == dest, 1.0, 0.0)
    seen = jnp.zeros((2 * members, 1), F32)
    ranks = []
    for first in range(0, obs_rows, LANES):
        part = member[:, first : first + LANES]
        count = jnp.dot(part.astype(BF16), upper, preferred_element_type=F32) + seen
        ranks.append(jnp.sum((count - 1.0) * part, axis=0, keepdims=True))
        seen = count[:, LANES - 1 :]
    rank = jnp.concatenate(ranks, axis=1).astype(jnp.int32)
    order_ref[0:1] = dest
    order_ref[1:2] = rank
    for copy in copies[1:]:
        copy.wait()
    start = foot_ref[0:1, :]
    meta = jnp.concatenate(
        [
            lax.div(start, cols).astype(F32),
            lax.rem(start, cols).astype(F32),
            weights_ref[...].astype(F32),
            jnp.zeros((META - 2 - weights_ref.shape[0], obs_rows), F32),
        ],
        axis=0,
    ).astype(BF16)
    meta_ref[...] = meta
    place(cap, members, dest, rank, meta, obs_ref[...], send_ref)


def near_kernel(cap, order_ref, meta_ref, obs_ref, send_ref):
    place(cap, 0, order_ref[0:1], order_ref[1:2], meta_ref[...], obs_ref[...], send_ref)


def gather_kernel(cap, cols, got_ref, field_ref):
    members, depth, _ = got_ref.shape
    cells, feats = field_ref.shape
    step = cols + 1
    per = LANES // cap
    halves = feats // LANES
    lane = lax.broadcasted_iota(jnp.int32, (META, LANES), 1)
    cell = lax.broadcasted_iota(jnp.int32, (cells, LANES), 0)
    total = jnp.zeros((cells, feats), F32)
    for pair in range(0, members // per, 2):
        maps = []
        blocks = []
        for chunk in (pair, pair + 1):
            meta = got_ref[chunk * per, depth - META :, :].astype(F32)
            for group in range(1, per):
                other = got_ref[chunk * per + group, depth - META :, :].astype(F32)
                meta = jnp.where(lane // cap == group, other, meta)
            start = (meta[0:1] * cols + meta[1:2]).astype(jnp.int32)
            away = cell - start
            away = jnp.where(away < 0, away + cells, away)
            amount = jnp.zeros((cells, LANES), F32)
            for entry in range(4):
                amount = jnp.where(away == entry * step, meta[2 + entry : 3 + entry], amount)
            maps.append(amount.astype(BF16))
            block = got_ref[chunk * per : (chunk + 1) * per]
            blocks.append(
                jnp.concatenate(
                    [
                        block[:, half * cap : (half + 1) * cap, :].reshape(LANES, LANES)
                        for half in range(halves)
                    ],
                    axis=1,
                )
            )
        total = total + jnp.dot(
            jnp.concatenate(maps, axis=1),
            jnp.concatenate(blocks, axis=0),
            preferred_element_type=F32,
        )
    field_ref[...] = total.astype(field_ref.dtype)


def state_kernel(near_ref, far_ref, proj_ref, back_ref, edge_ref, inner_ref, lon_ref, corner_ref):
    rows, cols, chans = back_ref.shape
    field = (near_ref[...] + far_ref[...].astype(F32)).astype(BF16)
    assim = jnp.dot(field, proj_ref[...], preferred_element_type=F32)
    state = back_ref[...].astype(F32) + assim.reshape(rows, cols, chans)
    state = state.astype(BF16)
    edge_ref[...] = state[rows - SHIFT :]
    inner_ref[...] = state[: rows - SHIFT]
    lon_ref[...] = state[:, cols - EDGE :, :]
    corner_ref[...] = state[rows - SHIFT :, cols - EDGE :, :]


def gelu(half):
    inner = half * (1.5957691216057308 + 0.285419265090401 * (half * half))
    return half + half * jnp.tanh(inner)


def put(wide_ref, row, start, value):
    for g in range(wide_ref.shape[0]):
        wide_ref[g, row, start : start + value.shape[0], :] = value[:, g * LANES : (g + 1) * LANES]


def shifted(wide_ref, taps_in, base, row, target):
    for g in range(wide_ref.shape[0]):
        for r in range(TAPS + 1):
            columns = pl.ds(base + r, TILE, stride=2)
            taps_in[g, r, target] = wide_ref[g, row, columns, :].astype(BF16)


def convolve(taps_in, taps_ref, tap_ref, spread_ref, layer, g, first, count):
    lanes = pl.ds(pl.multiple_of(g * LANES, LANES), LANES)
    for k in range(TAPS * TAPS):
        row = taps_ref[k, layer : layer + 1, lanes]
        tap_ref[k] = jnp.broadcast_to(row, (TILE, LANES)).astype(BF16)
    for p in range(2):
        total = None
        for b in range(TAPS):
            seen = taps_in[g, p + b, first : first + count + TAPS - 1]
            part = None
            for a in range(TAPS):
                term = seen[a : a + count] * tap_ref[a * TAPS + b]
                part = term if part is None else part + term
            total = part if total is None else total + part
        spread_ref[p, first : first + count, :, lanes] = total


def finish(taps_in, spread_ref, mix_ref, out_ref, layer, first, count):
    chans = mix_ref.shape[1]
    ones = jnp.ones((chans, LANES), BF16)
    for p in range(2):
        spread = spread_ref[p, first : first + count].reshape(count * TILE, chans)
        power = jnp.dot(spread * spread, ones, preferred_element_type=F32)
        scale = 0.5 * lax.rsqrt(power * (1.0 / chans) + 1e-05)
        mixed = jnp.dot(spread, mix_ref[layer], preferred_element_type=F32)
        for g in range(chans // LANES):
            moved = gelu(mixed[:, g * LANES : (g + 1) * LANES] * scale)
            center = taps_in[g, p + HALO, first + HALO : first + HALO + count].astype(F32)
            fresh = center + moved.reshape(count, TILE, LANES)
            for k in range(count):
                out_ref[g, first + k, pl.ds(p, TILE, stride=2), :] = fresh[k]


def row_of(out_ref, y):
    return jnp.concatenate([out_ref[g, y] for g in range(out_ref.shape[0])], axis=1)


def at_last():
    return lax.axis_index("lat") == lax.axis_size("lat") - 1


def inner_kernel(
    shrink,
    layer,
    edge_in,
    inner_in,
    lon_in,
    taps_ref,
    mix_ref,
    inner_ref,
    lon_ref,
    near_ref,
    wide_ref,
    taps_in,
    tap_ref,
    spread_ref,
    out_ref,
):
    cols = edge_in.shape[1]
    groups = wide_ref.shape[0]
    own = inner_in.shape[0] - (HALO if shrink else 0)
    rows = own + SHIFT
    count = rows - SHIFT
    side = cols if shrink else 0
    main = 0 if shrink else EDGE
    base = 0 if shrink else EDGE - SHIFT

    def load(ref, place, y):
        put(wide_ref, place, main, ref[y].astype(F32))
        put(wide_ref, place, side, lon_in[place].astype(F32))
        shifted(wide_ref, taps_in, base, place, place)

    @pl.loop(0, SHIFT, unroll=2)
    def _(y):
        load(edge_in, y if shrink else own + y, y)

    @pl.loop(0, own, unroll=2)
    def _(y):
        load(inner_in, y + SHIFT if shrink else y, y)

    near = rows - SHIFT if shrink else 0
    near_ref[...] = taps_in[:, :, near : near + SHIFT]

    @pl.loop(0, groups)
    def _(g):
        convolve(taps_in, taps_ref, tap_ref, spread_ref, layer, g, 0, count)

    finish(taps_in, spread_ref, mix_ref, out_ref, layer, 0, count)
    edge = slice(cols - EDGE, cols) if shrink else slice(0, EDGE)

    @pl.loop(0, count, unroll=2)
    def _(y):
        value = row_of(out_ref, y)
        inner_ref[y] = value.astype(BF16)
        lon_ref[y] = value[edge].astype(BF16)

    if not shrink:

        @pl.when(at_last())
        def _():
            taps_in[:, :, rows:] = jnp.zeros((groups, TAPS + 1, HALO, TILE, LANES), BF16)

            @pl.loop(0, groups)
            def _(g):
                convolve(taps_in, taps_ref, tap_ref, spread_ref, layer, g, count, HALO)

            finish(taps_in, spread_ref, mix_ref, out_ref, layer, count, HALO)

        for k in range(HALO):
            value = row_of(out_ref, count + k)
            inner_ref[count + k] = value.astype(BF16)
            lon_ref[count + k] = value[edge].astype(BF16)


def edge_kernel(
    shrink,
    final,
    layer,
    inner_in,
    lon_in,
    lat_in,
    corner_in,
    near_ref,
    inner_new,
    lon_new,
    taps_ref,
    mix_ref,
    *refs,
):
    if final:
        state_ref, wide_ref, taps_in, tap_ref, spread_ref, out_ref = refs
    else:
        edge_ref, lon_ref, corner_ref, wide_ref, taps_in, tap_ref, spread_ref, out_ref = refs
    cols = lat_in.shape[1]
    groups = wide_ref.shape[0]
    side = cols if shrink else 0
    main = 0 if shrink else EDGE
    base = 0 if shrink else EDGE - SHIFT
    last = at_last()
    top = lax.axis_index("lat") == 0
    own = SHIFT if not shrink else 0
    for k in range(SHIFT):
        value, beside = lat_in[k].astype(F32), corner_in[k].astype(F32)
        if not shrink:
            value, beside = jnp.where(top, 0.0, value), jnp.where(top, 0.0, beside)
        elif k < HALO:
            rows = lon_in.shape[0] - HALO
            kept = inner_in.shape[0] - HALO
            value = jnp.where(last, inner_in[kept + k].astype(F32), value)
            beside = jnp.where(last, lon_in[rows + k].astype(F32), beside)
        else:
            value, beside = jnp.where(last, 0.0, value), jnp.where(last, 0.0, beside)
        put(wide_ref, k, main, value)
        put(wide_ref, k, side, beside)
        shifted(wide_ref, taps_in, base, k, k if not shrink else k + SHIFT)
    taps_in[:, :, own : own + SHIFT] = near_ref[...]

    @pl.loop(0, groups)
    def _(g):
        convolve(taps_in, taps_ref, tap_ref, spread_ref, layer, g, 0, SHIFT)

    finish(taps_in, spread_ref, mix_ref, out_ref, layer, 0, SHIFT)
    kept = inner_new.shape[0]
    for k in range(SHIFT):
        value = row_of(out_ref, k)
        if final:
            state_ref[kept + k] = value.astype(BF16)
            continue
        if not shrink and k < HALO:
            value = jnp.where(top, 0.0, value)
        value = value.astype(F32)
        edge = value[cols - EDGE :] if shrink else value[:EDGE]
        edge_ref[k] = value.astype(BF16)
        corner_ref[k] = edge.astype(BF16)
        lon_ref[kept + k if shrink else k] = edge.astype(BF16)
    if final:
        state_ref[0:kept] = inner_new[...]
    elif shrink:
        lon_ref[0:kept] = lon_new[...]
    else:
        lon_ref[SHIFT : SHIFT + kept] = lon_new[...]


def call(kernel, out_shape, inputs, scratch=(), limit=VMEM_LIMIT, space=None, work=0):
    whole = pl.BlockSpec(memory_space=pltpu.VMEM)
    single = isinstance(out_shape, jax.ShapeDtypeStruct)
    spaces = space or (pltpu.VMEM,) * len(inputs)
    return pl.pallas_call(
        kernel,
        out_shape=out_shape,
        in_specs=[pl.BlockSpec(memory_space=s) for s in spaces],
        out_specs=whole if single else [whole] * len(out_shape),
        scratch_shapes=list(scratch),
        compiler_params=pltpu.CompilerParams(vmem_limit_bytes=limit),
        cost_estimate=pl.CostEstimate(flops=work, bytes_accessed=0, transcendentals=0),
    )(*inputs)


def held(*shape):
    return jax.ShapeDtypeStruct(shape, BF16)


def scratch_of(groups, seen, made, cols, chans):
    return (
        pltpu.VMEM((groups, seen, cols + EDGE, LANES), F32),
        pltpu.VMEM((groups, TAPS + 1, seen, TILE, LANES), BF16),
        pltpu.VMEM((TAPS * TAPS, TILE, LANES), BF16),
        pltpu.VMEM((2, made, TILE, chans), BF16),
        pltpu.VMEM((groups, made, cols, LANES), F32),
    )


def layer(state, lon_out, corner_out, taps, mix, number, shrink, final):
    edge, inner = state
    lat_in, lon_in, corner_in = exchange((edge, lon_out, corner_out), not shrink)
    cols, chans = edge.shape[1:]
    groups = chans // LANES
    rows = inner.shape[0] + SHIFT - (HALO if shrink else 0)
    spare = 0 if shrink else HALO
    made = rows - SHIFT + spare
    inner_new, lon_new, near = call(
        functools.partial(inner_kernel, shrink, number),
        (
            held(made, cols, chans),
            held(made, EDGE, chans),
            held(groups, TAPS + 1, SHIFT, TILE, LANES),
        ),
        (edge, inner, lon_in, taps, mix),
        scratch_of(groups, rows + spare, made, cols, chans),
        work=made * cols * chans * WORK,
    )
    if final:
        outs = held(made + SHIFT, cols, chans)
    else:
        outs = (
            held(SHIFT, cols, chans),
            held(made + SHIFT, EDGE, chans),
            held(SHIFT, EDGE, chans),
        )
    outs = call(
        functools.partial(edge_kernel, shrink, final, number),
        outs,
        (inner, lon_in, lat_in, corner_in, near, inner_new, lon_new, taps, mix),
        scratch_of(groups, 2 * SHIFT, SHIFT, cols, chans),
        work=SHIFT * cols * chans * WORK,
    )
    if final:
        return outs
    edge, lon_out, corner_out = outs
    return (edge, inner_new), lon_out, corner_out


def exchange(pieces, forward):
    lat, lon, corner = pieces
    count_lat = lax.axis_size("lat")
    count_lon = lax.axis_size("lon")
    along = [(i, (i + 1) % count_lat) for i in range(count_lat)]
    around = [(j, (j + 1) % count_lon) for j in range(count_lon)]
    across = [
        (i * count_lon + j, ni * count_lon + nj) for i, ni in along for j, nj in around
    ]
    if not forward:
        along, around, across = ([(t, s) for s, t in p] for p in (along, around, across))
    lon = lax.ppermute(lon, "lon", around)
    lat = lax.ppermute(lat, "lat", along)
    corner = lax.ppermute(corner, ("lat", "lon"), across)
    return lat, lon, corner


def body(
    background, observations, destination, footprint, weights, obs_proj, depth_w, point_w, gains
):
    rows, cols, chans = background.shape
    lat_count, lon_count = lax.axis_size("lat"), lax.axis_size("lon")
    obs_rows, feats = observations.shape
    cap = 2 * obs_rows // (lat_count * lon_count)
    depth = cap * (feats // LANES) + META
    foot_count = footprint.shape[1]
    half = lon_count // 2
    members = lat_count * half
    block = held(members, depth, LANES)
    send_far, order, meta = call(
        functools.partial(far_kernel, cap, cols, lon_count),
        (
            block,
            jax.ShapeDtypeStruct((2, obs_rows), jnp.int32),
            held(META, obs_rows),
        ),
        (destination.T, footprint.T, weights.T, observations),
        (
            pltpu.VMEM((1, obs_rows), jnp.int32),
            pltpu.VMEM((foot_count, obs_rows), jnp.int32),
            pltpu.VMEM((foot_count, obs_rows), BF16),
            pltpu.VMEM((obs_rows, feats), BF16),
            pltpu.SemaphoreType.DMA((4,)),
        ),
        PACK_LIMIT,
        (pltpu.HBM,) * 4,
        work=3 * MICROSECOND,
    )
    send_near = call(
        functools.partial(near_kernel, cap),
        block,
        (order, meta, observations),
        work=2 * MICROSECOND,
    )
    groups = [
        [i * lon_count + j for i in range(lat_count) for j in range(start, start + half)]
        for start in (0, half)
    ]
    got_far, got_near = (
        lax.all_to_all(
            send,
            ("lat", "lon"),
            split_axis=0,
            concat_axis=0,
            axis_index_groups=groups,
            tiled=True,
        )
        for send in (send_far, send_near)
    )
    cells = rows * cols
    far = call(
        functools.partial(gather_kernel, cap, cols),
        held(cells, feats),
        (got_far,),
        work=MICROSECOND,
    )
    far = lax.ppermute(far, "lon", [(j, (j + half) % lon_count) for j in range(lon_count)])
    near = call(
        functools.partial(gather_kernel, cap, cols),
        jax.ShapeDtypeStruct((cells, feats), F32),
        (got_near,),
        work=MICROSECOND,
    )
    layers = depth_w.shape[0]
    taps = depth_w.transpose(1, 2, 0, 3).reshape(TAPS * TAPS, layers, chans)
    mix = (gains[:, :, None] * point_w.astype(F32)).astype(BF16)
    near, mix = lax.optimization_barrier((near, mix))
    edge, inner, lon_out, corner_out = call(
        state_kernel,
        (
            held(SHIFT, cols, chans),
            held(rows - SHIFT, cols, chans),
            held(rows, EDGE, chans),
            held(SHIFT, EDGE, chans),
        ),
        (near, far, obs_proj, background),
        work=MICROSECOND,
    )
    state = (edge, inner)
    for n in range(layers - 1):
        state, lon_out, corner_out = layer(
            state, lon_out, corner_out, taps, mix, n, n % 2 == 1, False
        )
    n = layers - 1
    return layer(state, lon_out, corner_out, taps, mix, n, n % 2 == 1, True)


def solution(mesh):
    placed = (
        P("lat", "lon", None),
        P(("lat", "lon"), None),
        P(("lat", "lon"), None),
        P(("lat", "lon"), None),
        P(("lat", "lon"), None),
        P(),
        P(),
        P(),
        P(),
    )
    return jax.shard_map(
        body, mesh=mesh, in_specs=placed, out_specs=P("lat", "lon", None), check_vma=False
    )
```

profile of v0, /device:TPU:0, one launch (start us, length us, event | category | flops | bytes accessed | tf_op | source)
XLA Modules:
  0.0 92.8 jit_solution(5542005570148382058)
XLA Ops:
  0.0 3.5 %shard_map.91 = (bf16[16,136,128]{2,1,0:T(8,128)(2,1)}, s32[2,1024]{1,0:T(2,128)}, bf16[8,1024]{1,0:T(8,128)(2,1)}) custom-call(s32[1,1024]{1,0:T(1,128)} %bitcast.16, s32[4,1024]{1,0:T(4,128)} %bitcast.14, bf16[4,1024]{1,0:T(4,128)(2,1)} %bitcast.15, bf16[1024,256]{1,0:T(8,128)(2,1)} %obs_ref.1), custom_call_target="tpu_custom_call" | custom-call | flops 3449999872 | tf_op jit(solution)/shard_map/pallas_call | solution.py:391
  3.5 6.3 %all-to-all-start.1 = ((bf16[16,136,128]{2,1,0:T(8,128)(2,1)}), bf16[16,136,128]{2,1,0:T(8,128)(2,1)S(1)}, u32[]{:S(2)}, u32[]{:S(2)}) async-start(bf16[16,136,128]{2,1,0:T(8,128)(2,1)} %get-tuple-element.38), calls=%async_computation.1 | async-start | bytes 1114112 | tf_op jit(solution)/shard_map/all_to_all | solution.py:515
  11.2 2.1 %shard_map.92 = bf16[16,136,128]{2,1,0:T(8,128)(2,1)} custom-call(s32[2,1024]{1,0:T(2,128)S(1)} %copy-done.5, bf16[8,1024]{1,0:T(8,128)(2,1)S(1)} %copy-done.4, bf16[1024,256]{1,0:T(8,128)(2,1)S(1)} %copy-done), custom_call_target="tpu_custom_call" | custom-call | flops 2300000000 | tf_op jit(solution)/shard_map/pallas_call | solution.py:391
  13.3 7.4 %all-to-all-done.1.got_ref = bf16[16,136,128]{2,1,0:T(8,128)(2,1)S(1)} async-done(((bf16[16,136,128]{2,1,0:T(8,128)(2,1)}), bf16[16,136,128]{2,1,0:T(8,128)(2,1)S(1)}, u32[]{:S(2)}, u32[]{:S(2)}) %all-to-all-start.1) | async-done | bytes 557088 | tf_op jit(solution)/shard_map/all_to_all | solution.py:515
  20.7 3.6 %all-to-all-start = ((bf16[16,136,128]{2,1,0:T(8,128)(2,1)}), bf16[16,136,128]{2,1,0:T(8,128)(2,1)S(1)}, u32[]{:S(2)}, u32[]{:S(2)}) async-start(bf16[16,136,128]{2,1,0:T(8,128)(2,1)} %shard_map.92), calls=%async_computation | async-start | bytes 1114112 | tf_op jit(solution)/shard_map/all_to_all | solution.py:515
  24.3 1.7 %shard_map.94 = bf16[512,256]{1,0:T(8,128)(2,1)} custom-call(bf16[16,136,128]{2,1,0:T(8,128)(2,1)S(1)} %all-to-all-done.1.got_ref), custom_call_target="tpu_custom_call" | custom-call | flops 1150000000 | tf_op jit(solution)/shard_map/pallas_call | solution.py:391
  26.1 2.6 %collective-permute-start = (bf16[512,256]{1,0:T(8,128)(2,1)}, bf16[512,256]{1,0:T(8,128)(2,1)}, u32[]{:S(2)}, u32[]{:S(2)}) collective-permute-start(bf16[512,256]{1,0:T(8,128)(2,1)} %shard_map.94), channel_id=1, source_target_pairs={{0,4},{1,5},{2,6},{3,7},{4,0},{5,1},{6,2},{7,3},{8,12},{9,13},{10,... | collective-permute-start | bytes 786440 | tf_op jit(solution)/shard_map/ppermute | solution.py:532
  29.2 11.1 %all-to-all-done.got_ref = bf16[16,136,128]{2,1,0:T(8,128)(2,1)S(1)} async-done(((bf16[16,136,128]{2,1,0:T(8,128)(2,1)}), bf16[16,136,128]{2,1,0:T(8,128)(2,1)S(1)}, u32[]{:S(2)}, u32[]{:S(2)}) %all-to-all-start) | async-done | bytes 557088 | tf_op jit(solution)/shard_map/all_to_all | solution.py:515
  42.8 2.1 %collective-permute-start.3 = (bf16[6,8,512]{2,1,0:T(8,128)(2,1)S(1)}, bf16[6,8,512]{2,1,0:T(8,128)(2,1)S(1)}, u32[]{:S(2)}, u32[]{:S(2)}) collective-permute-start(bf16[6,8,512]{2,1,0:T(8,128)(2,1)S(1)} %get-tuple-element.44), channel_id=1, source_target_pairs={{0,9},{1,10},{2,11},{3,12},{4,13},{5,14},{6,15},{7,8},{8,17},{9,18... | collective-permute-start | bytes 147464 | tf_op jit(solution)/shard_map/ppermute | solution.py:469
  46.3 2.6 %collective-permute-done.1.lon_in = bf16[16,8,512]{2,1,0:T(8,128)(2,1)S(1)} collective-permute-done((bf16[16,8,512]{2,1,0:T(8,128)(2,1)S(1)}, bf16[16,8,512]{2,1,0:T(8,128)(2,1)S(1)}, u32[]{:S(2)}, u32[]{:S(2)}) %collective-permute-start.1) | collective-permute-done | bytes 131104 | tf_op jit(solution)/shard_map/ppermute | solution.py:467
  48.9 3.2 %shard_map.96 = (bf16[13,32,512]{2,1,0:T(8,128)(2,1)S(1)}, bf16[13,8,512]{2,1,0:T(8,128)(2,1)S(1)}, bf16[4,8,6,16,128]{4,3,2,1,0:T(8,128)(2,1)S(1)}) custom-call(bf16[6,32,512]{2,1,0:T(8,128)(2,1)S(1)} %get-tuple-element.39.edge_in, bf16[10,32,512]{2,1,0:T(8,128)(2,1)S(1)} %get-tuple-element.40.inner_in, ...), custom_call_target="tpu_custom_call" | custom-call | flops 8519680000 | tf_op jit(solution)/shard_map/pallas_call | solution.py:391
  53.1 2.0 %shard_map.97 = (bf16[6,32,512]{2,1,0:T(8,128)(2,1)S(1)}, bf16[19,8,512]{2,1,0:T(8,128)(2,1)S(1)}, bf16[6,8,512]{2,1,0:T(8,128)(2,1)S(1)}) custom-call(bf16[10,32,512]{2,1,0:T(8,128)(2,1)S(1)} %get-tuple-element.40.inner_in, bf16[16,8,512]{2,1,0:T(8,128)(2,1)S(1)} %collective-permute-done.1.lon_in, bf16[6,32,512]{2,1,0:T(8,128)(2,1)S(1)} %collective-permute-done.2.lat_in, ...), custom_call_target="tpu_custom_call" | custom-call | flops 3932160000 | tf_op jit(solution)/shard_map/pallas_call | solution.py:391
  55.1 1.7 %collective-permute-start.4 = (bf16[19,8,512]{2,1,0:T(8,128)(2,1)S(1)}, bf16[19,8,512]{2,1,0:T(8,128)(2,1)S(1)}, u32[]{:S(2)}, u32[]{:S(2)}) collective-permute-start(bf16[19,8,512]{2,1,0:T(8,128)(2,1)S(1)} %get-tuple-element.47), channel_id=1, source_target_pairs={{1,0},{2,1},{3,2},{4,3},{5,4},{6,5},{7,6},{0,7},{9,8},{10,9},{11,1... | collective-permute-start | bytes 466952 | tf_op jit(solution)/shard_map/ppermute | solution.py:467
  56.8 2.5 %collective-permute-start.6 = (bf16[6,8,512]{2,1,0:T(8,128)(2,1)S(1)}, bf16[6,8,512]{2,1,0:T(8,128)(2,1)S(1)}, u32[]{:S(2)}, u32[]{:S(2)}) collective-permute-start(bf16[6,8,512]{2,1,0:T(8,128)(2,1)S(1)} %get-tuple-element.49), channel_id=1, source_target_pairs={{9,0},{10,1},{11,2},{12,3},{13,4},{14,5},{15,6},{8,7},{17,8},{18,9... | collective-permute-start | bytes 147464 | tf_op jit(solution)/shard_map/ppermute | solution.py:469
  60.8 3.3 %shard_map.98 = (bf16[10,32,512]{2,1,0:T(8,128)(2,1)S(1)}, bf16[10,8,512]{2,1,0:T(8,128)(2,1)S(1)}, bf16[4,8,6,16,128]{4,3,2,1,0:T(8,128)(2,1)S(1)}) custom-call(bf16[6,32,512]{2,1,0:T(8,128)(2,1)S(1)} %get-tuple-element.48.edge_in, bf16[13,32,512]{2,1,0:T(8,128)(2,1)S(1)} %get-tuple-element.43.inner_new.inner_in, ...), custom_call_target="tpu_custom_call" | custom-call | flops 6553600000 | tf_op jit(solution)/shard_map/pallas_call | solution.py:391
  65.0 2.0 %shard_map.99 = (bf16[6,32,512]{2,1,0:T(8,128)(2,1)S(1)}, bf16[16,8,512]{2,1,0:T(8,128)(2,1)S(1)}, bf16[6,8,512]{2,1,0:T(8,128)(2,1)S(1)}) custom-call(bf16[13,32,512]{2,1,0:T(8,128)(2,1)S(1)} %get-tuple-element.43.inner_new.inner_in, bf16[19,8,512]{2,1,0:T(8,128)(2,1)S(1)} %collective-permute-done.4.lon_in, ...), custom_call_target="tpu_custom_call" | custom-call | flops 3932160000 | tf_op jit(solution)/shard_map/pallas_call | solution.py:391
  69.2 4.1 %collective-permute-done.7.lon_in = bf16[16,8,512]{2,1,0:T(8,128)(2,1)S(1)} collective-permute-done((bf16[16,8,512]{2,1,0:T(8,128)(2,1)S(1)}, bf16[16,8,512]{2,1,0:T(8,128)(2,1)S(1)}, u32[]{:S(2)}, u32[]{:S(2)}) %collective-permute-start.7) | collective-permute-done | bytes 131104 | tf_op jit(solution)/shard_map/ppermute | solution.py:467
  73.2 3.2 %shard_map.100 = (bf16[13,32,512]{2,1,0:T(8,128)(2,1)S(1)}, bf16[13,8,512]{2,1,0:T(8,128)(2,1)S(1)}, bf16[4,8,6,16,128]{4,3,2,1,0:T(8,128)(2,1)S(1)}) custom-call(bf16[6,32,512]{2,1,0:T(8,128)(2,1)S(1)} %get-tuple-element.53.edge_in, bf16[10,32,512]{2,1,0:T(8,128)(2,1)S(1)} %get-tuple-element.51.inner_new.inner_in, ...), custom_call_target="tpu_custom_call" | custom-call | flops 8519680000 | tf_op jit(solution)/shard_map/pallas_call | solution.py:391
  76.7 2.0 %shard_map.101 = (bf16[6,32,512]{2,1,0:T(8,128)(2,1)S(1)}, bf16[19,8,512]{2,1,0:T(8,128)(2,1)S(1)}, bf16[6,8,512]{2,1,0:T(8,128)(2,1)S(1)}) custom-call(bf16[10,32,512]{2,1,0:T(8,128)(2,1)S(1)} %get-tuple-element.51.inner_new.inner_in, bf16[16,8,512]{2,1,0:T(8,128)(2,1)S(1)} %collective-permute-done.7.lon_in, ...), custom_call_target="tpu_custom_call" | custom-call | flops 3932160000 | tf_op jit(solution)/shard_map/pallas_call | solution.py:391
  78.6 2.7 %collective-permute-start.10 = (bf16[19,8,512]{2,1,0:T(8,128)(2,1)S(1)}, bf16[19,8,512]{2,1,0:T(8,128)(2,1)S(1)}, u32[]{:S(2)}, u32[]{:S(2)}) collective-permute-start(bf16[19,8,512]{2,1,0:T(8,128)(2,1)S(1)} %get-tuple-element.59), channel_id=1, source_target_pairs={{1,0},{2,1},{3,2},{4,3},{5,4},{6,5},{7,6},{0,7},{9,8},{10,9},{11,1... | collective-permute-start | bytes 466952 | tf_op jit(solution)/shard_map/ppermute | solution.py:467
  81.3 2.0 %collective-permute-start.12 = (bf16[6,8,512]{2,1,0:T(8,128)(2,1)S(1)}, bf16[6,8,512]{2,1,0:T(8,128)(2,1)S(1)}, u32[]{:S(2)}, u32[]{:S(2)}) collective-permute-start(bf16[6,8,512]{2,1,0:T(8,128)(2,1)S(1)} %get-tuple-element.61), channel_id=1, source_target_pairs={{9,0},{10,1},{11,2},{12,3},{13,4},{14,5},{15,6},{8,7},{17,8},{18,9... | collective-permute-start | bytes 147464 | tf_op jit(solution)/shard_map/ppermute | solution.py:469
  83.3 1.9 %collective-permute-start.11 = (bf16[6,32,512]{2,1,0:T(8,128)(2,1)S(1)}, bf16[6,32,512]{2,1,0:T(8,128)(2,1)S(1)}, u32[]{:S(2)}, u32[]{:S(2)}) collective-permute-start(bf16[6,32,512]{2,1,0:T(8,128)(2,1)S(1)} %get-tuple-element.60.edge_in), channel_id=1, source_target_pairs={{8,0},{16,8},{24,16},{0,24},{9,1},{17,9},{25,17},{1,25},{10,2},{18... | collective-permute-start | bytes 589832 | tf_op jit(solution)/shard_map/ppermute | solution.py:468
  85.2 3.3 %shard_map.102 = (bf16[10,32,512]{2,1,0:T(8,128)(2,1)S(1)}, bf16[10,8,512]{2,1,0:T(8,128)(2,1)S(1)}, bf16[4,8,6,16,128]{4,3,2,1,0:T(8,128)(2,1)S(1)}) custom-call(bf16[6,32,512]{2,1,0:T(8,128)(2,1)S(1)} %get-tuple-element.60.edge_in, bf16[13,32,512]{2,1,0:T(8,128)(2,1)S(1)} %get-tuple-element.55.inner_new.inner_in, ...), custom_call_target="tpu_custom_call" | custom-call | flops 6553600000 | tf_op jit(solution)/shard_map/pallas_call | solution.py:391
  90.0 2.8 %shard_map.103 = bf16[16,32,512]{2,1,0:T(8,128)(2,1)} custom-call(bf16[13,32,512]{2,1,0:T(8,128)(2,1)S(1)} %get-tuple-element.55.inner_new.inner_in, bf16[19,8,512]{2,1,0:T(8,128)(2,1)S(1)} %collective-permute-done.10.lon_in, bf16[6,32,512]{2,1,0:T(8,128)(2,1)S(1)} %collective-permute-done.11.lat_in, ...), custom_call_target="tpu_custom_call" | custom-call | flops 3932160000 | tf_op jit(solution)/shard_map/pallas_call | solution.py:391
  (36 shorter events, 13.0 us)
Async XLA Ops:
  0.0 9.8 %copy-start = (bf16[1024,256]{1,0:T(8,128)(2,1)S(1)}, bf16[1024,256]{1,0:T(8,128)(2,1)}, u32[]{:S(2)}) copy-start(bf16[1024,256]{1,0:T(8,128)(2,1)} %obs_ref.1) | copy-start | bytes 1572868
  3.5 17.2 %all-to-all-start.1 = ((bf16[16,136,128]{2,1,0:T(8,128)(2,1)}), bf16[16,136,128]{2,1,0:T(8,128)(2,1)S(1)}, u32[]{:S(2)}, u32[]{:S(2)}) async-start(bf16[16,136,128]{2,1,0:T(8,128)(2,1)} %get-tuple-element.38), calls=%async_computation.1 | async-start | bytes 1114112 | tf_op jit(solution)/shard_map/all_to_all | solution.py:515
  9.8 0.7 copy-start.4
  10.5 0.7 copy-start.5
  20.7 19.6 %all-to-all-start = ((bf16[16,136,128]{2,1,0:T(8,128)(2,1)}), bf16[16,136,128]{2,1,0:T(8,128)(2,1)S(1)}, u32[]{:S(2)}, u32[]{:S(2)}) async-start(bf16[16,136,128]{2,1,0:T(8,128)(2,1)} %shard_map.92), calls=%async_computation | async-start | bytes 1114112 | tf_op jit(solution)/shard_map/all_to_all | solution.py:515
  24.3 4.4 %copy-start.6 = (bf16[4,512,512]{2,1,0:T(8,128)(2,1)S(1)}, bf16[4,512,512]{2,1,0:T(8,128)(2,1)}, u32[]{:S(2)}) copy-start(bf16[4,512,512]{2,1,0:T(8,128)(2,1)} %param.16) | copy-start | bytes 6291460
  24.3 4.4 %copy-start.7 = (f32[4,512]{1,0:T(4,128)S(1)}, f32[4,512]{1,0:T(4,128)}, u32[]{:S(2)}) copy-start(f32[4,512]{1,0:T(4,128)} %param.17) | copy-start | bytes 24580
  26.1 15.4 %collective-permute-start = (bf16[512,256]{1,0:T(8,128)(2,1)}, bf16[512,256]{1,0:T(8,128)(2,1)}, u32[]{:S(2)}, u32[]{:S(2)}) collective-permute-start(bf16[512,256]{1,0:T(8,128)(2,1)} %shard_map.94), channel_id=1, source_target_pairs={{0,4},{1,5},{2,6},{3,7},{4,0},{5,1},{6,2},{7,3},{8,12},{9,13},{10,... | collective-permute-start | bytes 786440 | tf_op jit(solution)/shard_map/ppermute | solution.py:532
  29.1 12.3 %copy-start.1 = (bf16[16,32,512]{2,1,0:T(8,128)(2,1)S(1)}, bf16[16,32,512]{2,1,0:T(8,128)(2,1)}, u32[]{:S(2)}) copy-start(bf16[16,32,512]{2,1,0:T(8,128)(2,1)} %back_ref.1) | copy-start | bytes 1572868
  29.1 12.3 %copy-start.3 = (bf16[256,512]{1,0:T(8,128)(2,1)S(1)}, bf16[256,512]{1,0:T(8,128)(2,1)}, u32[]{:S(2)}) copy-start(bf16[256,512]{1,0:T(8,128)(2,1)} %proj_ref.1) | copy-start | bytes 786436
  41.3 7.6 %copy-start.2 = (f32[4,7,7,512]{3,0,2,1:T(4,128)S(1)}, f32[4,7,7,512]{3,0,2,1:T(4,128)}, u32[]{:S(2)}) copy-start(f32[4,7,7,512]{3,0,2,1:T(4,128)} %param.15) | copy-start | bytes 1204228
  42.7 6.2 %collective-permute-start.1 = (bf16[16,8,512]{2,1,0:T(8,128)(2,1)S(1)}, bf16[16,8,512]{2,1,0:T(8,128)(2,1)S(1)}, u32[]{:S(2)}, u32[]{:S(2)}) collective-permute-start(bf16[16,8,512]{2,1,0:T(8,128)(2,1)S(1)} %get-tuple-element.41), channel_id=1, source_target_pairs={{0,1},{1,2},{2,3},{3,4},{4,5},{5,6},{6,7},{7,0},{8,9},{9,10},{10,1... | collective-permute-start | bytes 393224 | tf_op jit(solution)/shard_map/ppermute | solution.py:467
  42.8 9.4 %collective-permute-start.3 = (bf16[6,8,512]{2,1,0:T(8,128)(2,1)S(1)}, bf16[6,8,512]{2,1,0:T(8,128)(2,1)S(1)}, u32[]{:S(2)}, u32[]{:S(2)}) collective-permute-start(bf16[6,8,512]{2,1,0:T(8,128)(2,1)S(1)} %get-tuple-element.44), channel_id=1, source_target_pairs={{0,9},{1,10},{2,11},{3,12},{4,13},{5,14},{6,15},{7,8},{8,17},{9,18... | collective-permute-start | bytes 147464 | tf_op jit(solution)/shard_map/ppermute | solution.py:469
  44.8 8.2 %collective-permute-start.2 = (bf16[6,32,512]{2,1,0:T(8,128)(2,1)S(1)}, bf16[6,32,512]{2,1,0:T(8,128)(2,1)S(1)}, u32[]{:S(2)}, u32[]{:S(2)}) collective-permute-start(bf16[6,32,512]{2,1,0:T(8,128)(2,1)S(1)} %get-tuple-element.39.edge_in), channel_id=1, source_target_pairs={{0,8},{8,16},{16,24},{24,0},{1,9},{9,17},{17,25},{25,1},{2,10},{10... | collective-permute-start | bytes 589832 | tf_op jit(solution)/shard_map/ppermute | solution.py:468
  55.1 5.8 %collective-permute-start.4 = (bf16[19,8,512]{2,1,0:T(8,128)(2,1)S(1)}, bf16[19,8,512]{2,1,0:T(8,128)(2,1)S(1)}, u32[]{:S(2)}, u32[]{:S(2)}) collective-permute-start(bf16[19,8,512]{2,1,0:T(8,128)(2,1)S(1)} %get-tuple-element.47), channel_id=1, source_target_pairs={{1,0},{2,1},{3,2},{4,3},{5,4},{6,5},{7,6},{0,7},{9,8},{10,9},{11,1... | collective-permute-start | bytes 466952 | tf_op jit(solution)/shard_map/ppermute | solution.py:467
  56.8 7.4 %collective-permute-start.6 = (bf16[6,8,512]{2,1,0:T(8,128)(2,1)S(1)}, bf16[6,8,512]{2,1,0:T(8,128)(2,1)S(1)}, u32[]{:S(2)}, u32[]{:S(2)}) collective-permute-start(bf16[6,8,512]{2,1,0:T(8,128)(2,1)S(1)} %get-tuple-element.49), channel_id=1, source_target_pairs={{9,0},{10,1},{11,2},{12,3},{13,4},{14,5},{15,6},{8,7},{17,8},{18,9... | collective-permute-start | bytes 147464 | tf_op jit(solution)/shard_map/ppermute | solution.py:469
  59.3 5.7 %collective-permute-start.5 = (bf16[6,32,512]{2,1,0:T(8,128)(2,1)S(1)}, bf16[6,32,512]{2,1,0:T(8,128)(2,1)S(1)}, u32[]{:S(2)}, u32[]{:S(2)}) collective-permute-start(bf16[6,32,512]{2,1,0:T(8,128)(2,1)S(1)} %get-tuple-element.48.edge_in), channel_id=1, source_target_pairs={{8,0},{16,8},{24,16},{0,24},{9,1},{17,9},{25,17},{1,25},{10,2},{18... | collective-permute-start | bytes 589832 | tf_op jit(solution)/shard_map/ppermute | solution.py:468
  67.0 6.2 %collective-permute-start.7 = (bf16[16,8,512]{2,1,0:T(8,128)(2,1)S(1)}, bf16[16,8,512]{2,1,0:T(8,128)(2,1)S(1)}, u32[]{:S(2)}, u32[]{:S(2)}) collective-permute-start(bf16[16,8,512]{2,1,0:T(8,128)(2,1)S(1)} %get-tuple-element.54), channel_id=1, source_target_pairs={{0,1},{1,2},{2,3},{3,4},{4,5},{5,6},{6,7},{7,0},{8,9},{9,10},{10,1... | collective-permute-start | bytes 393224 | tf_op jit(solution)/shard_map/ppermute | solution.py:467
  67.0 9.6 %collective-permute-start.9 = (bf16[6,8,512]{2,1,0:T(8,128)(2,1)S(1)}, bf16[6,8,512]{2,1,0:T(8,128)(2,1)S(1)}, u32[]{:S(2)}, u32[]{:S(2)}) collective-permute-start(bf16[6,8,512]{2,1,0:T(8,128)(2,1)S(1)} %get-tuple-element.56), channel_id=1, source_target_pairs={{0,9},{1,10},{2,11},{3,12},{4,13},{5,14},{6,15},{7,8},{8,17},{9,18... | collective-permute-start | bytes 147464 | tf_op jit(solution)/shard_map/ppermute | solution.py:469
  68.0 8.7 %collective-permute-start.8 = (bf16[6,32,512]{2,1,0:T(8,128)(2,1)S(1)}, bf16[6,32,512]{2,1,0:T(8,128)(2,1)S(1)}, u32[]{:S(2)}, u32[]{:S(2)}) collective-permute-start(bf16[6,32,512]{2,1,0:T(8,128)(2,1)S(1)} %get-tuple-element.53.edge_in), channel_id=1, source_target_pairs={{0,8},{8,16},{16,24},{24,0},{1,9},{9,17},{17,25},{25,1},{2,10},{10... | collective-permute-start | bytes 589832 | tf_op jit(solution)/shard_map/ppermute | solution.py:468
  78.6 6.5 %collective-permute-start.10 = (bf16[19,8,512]{2,1,0:T(8,128)(2,1)S(1)}, bf16[19,8,512]{2,1,0:T(8,128)(2,1)S(1)}, u32[]{:S(2)}, u32[]{:S(2)}) collective-permute-start(bf16[19,8,512]{2,1,0:T(8,128)(2,1)S(1)} %get-tuple-element.59), channel_id=1, source_target_pairs={{1,0},{2,1},{3,2},{4,3},{5,4},{6,5},{7,6},{0,7},{9,8},{10,9},{11,1... | collective-permute-start | bytes 466952 | tf_op jit(solution)/shard_map/ppermute | solution.py:467
  81.3 7.2 %collective-permute-start.12 = (bf16[6,8,512]{2,1,0:T(8,128)(2,1)S(1)}, bf16[6,8,512]{2,1,0:T(8,128)(2,1)S(1)}, u32[]{:S(2)}, u32[]{:S(2)}) collective-permute-start(bf16[6,8,512]{2,1,0:T(8,128)(2,1)S(1)} %get-tuple-element.61), channel_id=1, source_target_pairs={{9,0},{10,1},{11,2},{12,3},{13,4},{14,5},{15,6},{8,7},{17,8},{18,9... | collective-permute-start | bytes 147464 | tf_op jit(solution)/shard_map/ppermute | solution.py:469
  83.3 6.7 %collective-permute-start.11 = (bf16[6,32,512]{2,1,0:T(8,128)(2,1)S(1)}, bf16[6,32,512]{2,1,0:T(8,128)(2,1)S(1)}, u32[]{:S(2)}, u32[]{:S(2)}) collective-permute-start(bf16[6,32,512]{2,1,0:T(8,128)(2,1)S(1)} %get-tuple-element.60.edge_in), channel_id=1, source_target_pairs={{8,0},{16,8},{24,16},{0,24},{9,1},{17,9},{25,17},{1,25},{10,2},{18... | collective-permute-start | bytes 589832 | tf_op jit(solution)/shard_map/ppermute | solution.py:468
where the time goes:
time: 93.2 us; the launch traced here: 92.8 us
  Pallas kernels  31.4 us (34%)
  starting transfers between devices  30.5 us (33%)
  waiting for transfers between devices  28.7 us (31%)
  local copies, waits for them, and re-layouts  1.44 us (2%)
    pallas_call x13, Pallas kernels, call(): pl.pallas_call(kernel, out_shape=out_shape, in_specs=[pl.BlockSpec(memory...  31.4 us
    all_to_all x2, waiting for transfers between devices, body(): lax.all_to_all(send, ('lat', 'lon'), split_axis=0, concat_axis=0, axis_in...  18.5 us
    all_to_all x2, starting transfers between devices, body(): lax.all_to_all(send, ('lat', 'lon'), split_axis=0, concat_axis=0, axis_in...  9.88 us
    ppermute x4, starting transfers between devices, exchange(): corner = lax.ppermute(corner, ('lat', 'lon'), across)  7.5 us
    ppermute x4, waiting for transfers between devices, exchange(): lon = lax.ppermute(lon, 'lon', around)  6.66 us
    ppermute x4, starting transfers between devices, exchange(): lat = lax.ppermute(lat, 'lat', along)  6.07 us
    ppermute x4, starting transfers between devices, exchange(): lon = lax.ppermute(lon, 'lon', around)  4.51 us
    ppermute x4, waiting for transfers between devices, exchange(): lat = lax.ppermute(lat, 'lat', along)  3.24 us
  transfers between devices with their start and end apart: 15, of which 9 were waited for; matrix products, arithmetic and copies ran while one was open for 0% of the time, Pallas kernels for 19%

commit v1 on v0

--- a/solution.py
+++ b/solution.py
@@ -15,7 +15,7 @@
 EDGE = 8
 TILE = 16
 MICROSECOND = 1150000000
-WORK = 40000
+WORK = 5000
 VMEM_LIMIT = 24 * 1024 * 1024
 PACK_LIMIT = 58 * 1024 * 1024
 BF16 = jnp.bfloat16
@@ -126,7 +126,8 @@
     place(cap, members, dest, rank, meta, obs_ref[...], send_ref)
 
 
-def near_kernel(cap, order_ref, meta_ref, obs_ref, send_ref):
+def near_kernel(cap, order_ref, meta_ref, obs_ref, after_ref, send_ref):
+    del after_ref
     place(cap, 0, order_ref[0:1], order_ref[1:2], meta_ref[...], obs_ref[...], send_ref)
 
 
@@ -501,35 +502,35 @@
         (pltpu.HBM,) * 4,
         work=3 * MICROSECOND,
     )
-    send_near = call(
-        functools.partial(near_kernel, cap),
-        block,
-        (order, meta, observations),
-        work=2 * MICROSECOND,
-    )
     groups = [
         [i * lon_count + j for i in range(lat_count) for j in range(start, start + half)]
         for start in (0, half)
     ]
-    got_far, got_near = (
-        lax.all_to_all(
-            send,
-            ("lat", "lon"),
-            split_axis=0,
-            concat_axis=0,
-            axis_index_groups=groups,
-            tiled=True,
-        )
-        for send in (send_far, send_near)
-    )
+    exchanged = functools.partial(
+        lax.all_to_all,
+        axis_name=("lat", "lon"),
+        split_axis=0,
+        concat_axis=0,
+        axis_index_groups=groups,
+        tiled=True,
+    )
+    got_far = exchanged(send_far)
     cells = rows * cols
-    far = call(
+    field = call(
         functools.partial(gather_kernel, cap, cols),
         held(cells, feats),
         (got_far,),
         work=MICROSECOND,
     )
-    far = lax.ppermute(far, "lon", [(j, (j + half) % lon_count) for j in range(lon_count)])
+    far = lax.ppermute(field, "lon", [(j, (j + half) % lon_count) for j in range(lon_count)])
+    send_near = call(
+        functools.partial(near_kernel, cap),
+        block,
+        (order, meta, observations, field),
+        space=(pltpu.VMEM, pltpu.VMEM, pltpu.VMEM, pl.ANY),
+        work=2 * MICROSECOND,
+    )
+    got_near = exchanged(send_near)
     near = call(
         functools.partial(gather_kernel, cap, cols),
         jax.ShapeDtypeStruct((cells, feats), F32),

time: 93.2 us -> 93.1 us (level)
  blocking collectives: 0 us -> 17.2 us
  starting transfers between devices: 30.5 us -> 17.4 us
  waiting for transfers between devices: 28.7 us -> 24.3 us
  other arithmetic: 0.46 us -> 2.05 us
  local copies, waits for them, and re-layouts: 1.44 us -> 0.03 us
    all_to_all x0 -> x1, blocking collectives: none -> 17.2 us  [body(): got_far = exchanged(send_far)]
    all_to_all x2 -> x1, waiting for transfers between devices: 18.5 us -> 11.7 us  [body(): got_near = exchanged(send_near)]
    all_to_all x2 -> x1, starting transfers between devices: 9.88 us -> 3.58 us  [body(): got_near = exchanged(send_near)]
    ppermute x4, waiting for transfers between devices: 6.66 us -> 10.8 us  [exchange(): lon = lax.ppermute(lon, 'lon', around)]
    ppermute x4, starting transfers between devices: 7.5 us -> 3.7 us  [exchange(): corner = lax.ppermute(corner, ('lat', 'lon'), across)]
    ppermute x4, starting transfers between devices: 6.07 us -> 3.34 us  [exchange(): lat = lax.ppermute(lat, 'lat', along)]
    convert_element_type x1, other arithmetic: 0.46 us -> 2.05 us  [body(): mix = (gains[:, :, None] * point_w.astype(F32)).astype(BF16)]
    ppermute x4, waiting for transfers between devices: 3.24 us -> 1.76 us  [exchange(): lat = lax.ppermute(lat, 'lat', along)]
  transfers between devices with their start and end apart: 15 -> 14, of which waited for: 9 -> 7; matrix products, arithmetic and copies ran while one was open for 0% -> 2% of each run, Pallas kernels for 19% -> 15%
where the time goes in v1:
time: 93.1 us; the launch traced here: 92.7 us
  Pallas kernels  31.5 us (34%)
  waiting for transfers between devices  24.3 us (26%)
  starting transfers between devices  17.4 us (19%)
  blocking collectives  17.2 us (18%)
  other arithmetic  2.05 us (2%)
    pallas_call x13, Pallas kernels, call(): pl.pallas_call(kernel, out_shape=out_shape, in_specs=[pl.BlockSpec(memory...  31.5 us
    all_to_all x1, blocking collectives, body(): got_far = exchanged(send_far)  17.2 us
    all_to_all x1, waiting for transfers between devices, body(): got_near = exchanged(send_near)  11.7 us
    ppermute x4, waiting for transfers between devices, exchange(): lon = lax.ppermute(lon, 'lon', around)  10.8 us
    ppermute x4, starting transfers between devices, exchange(): lon = lax.ppermute(lon, 'lon', around)  4.13 us
    ppermute x4, starting transfers between devices, exchange(): corner = lax.ppermute(corner, ('lat', 'lon'), across)  3.7 us
    all_to_all x1, starting transfers between devices, body(): got_near = exchanged(send_near)  3.58 us
    ppermute x4, starting transfers between devices, exchange(): lat = lax.ppermute(lat, 'lat', along)  3.34 us
  transfers between devices with their start and end apart: 14, of which 7 were waited for; matrix products, arithmetic and copies ran while one was open for 2% of the time, Pallas kernels for 15%

profile of v1, /device:TPU:0, one launch (start us, length us, event | category | flops | bytes accessed | tf_op | source)
XLA Modules:
  0.0 92.7 jit_solution(2593207209918534292)
XLA Ops:
  0.0 3.5 %shard_map.91 = (bf16[16,136,128]{2,1,0:T(8,128)(2,1)}, s32[2,1024]{1,0:T(2,128)}, bf16[8,1024]{1,0:T(8,128)(2,1)}) custom-call(s32[1,1024]{1,0:T(1,128)} %bitcast.16, s32[4,1024]{1,0:T(4,128)} %bitcast.14, bf16[4,1024]{1,0:T(4,128)(2,1)} %bitcast.15, bf16[1024,256]{1,0:T(8,128)(2,1)} %obs_ref.1), custom_call_target="tpu_custom_call" | custom-call | flops 3449999872 | tf_op jit(solution)/shard_map/pallas_call | solution.py:392
  3.5 17.2 %all_to_all.10.got_ref = bf16[16,136,128]{2,1,0:T(8,128)(2,1)S(1)} all-to-all(bf16[16,136,128]{2,1,0:T(8,128)(2,1)} %get-tuple-element.37), channel_id=1, replica_groups={{0,1,2,3,8,9,10,11,16,17,18,19,24,25,26,27},{4,5,6,7,12,13,14,15,20,21,..., dimensions={0} | all-to-all | bytes 1114112 | tf_op jit(solution)/shard_map/all_to_all | solution.py:517
  20.7 1.7 %shard_map.92.after_ref = bf16[512,256]{1,0:T(8,128)(2,1)} custom-call(bf16[16,136,128]{2,1,0:T(8,128)(2,1)S(1)} %all_to_all.10.got_ref), custom_call_target="tpu_custom_call" | custom-call | flops 1150000000 | tf_op jit(solution)/shard_map/pallas_call | solution.py:392
  22.4 2.1 %shard_map.93 = bf16[16,136,128]{2,1,0:T(8,128)(2,1)} custom-call(s32[2,1024]{1,0:T(2,128)S(1)} %copy-done.5, bf16[8,1024]{1,0:T(8,128)(2,1)S(1)} %copy-done.4, bf16[1024,256]{1,0:T(8,128)(2,1)S(1)} %copy-done.1, bf16[512,256]{1,0:T(8,128)(2,1)} %shard_map.92.after_ref), custom_call_target="tpu_custom_call" | custom-call | flops 2300000000 | tf_op jit(solution)/shard_map/pallas_call | solution.py:392
  24.5 3.6 %all-to-all-start.1 = ((bf16[16,136,128]{2,1,0:T(8,128)(2,1)}), bf16[16,136,128]{2,1,0:T(8,128)(2,1)S(1)}, u32[]{:S(2)}, u32[]{:S(2)}) async-start(bf16[16,136,128]{2,1,0:T(8,128)(2,1)} %shard_map.93), calls=%async_computation.1 | async-start | bytes 1114112 | tf_op jit(solution)/shard_map/all_to_all | solution.py:533
  28.1 2.7 %collective-permute-start = (bf16[512,256]{1,0:T(8,128)(2,1)}, bf16[512,256]{1,0:T(8,128)(2,1)}, u32[]{:S(2)}, u32[]{:S(2)}) collective-permute-start(bf16[512,256]{1,0:T(8,128)(2,1)} %shard_map.92.after_ref), channel_id=1, source_target_pairs={{0,4},{1,5},{2,6},{3,7},{4,0},{5,1},{6,2},{7,3},{8,12},{9,13},{10,... | collective-permute-start | bytes 786440 | tf_op jit(solution)/shard_map/ppermute | solution.py:525
  30.8 2.0 %multiply_convert_fusion.mix_ref = bf16[4,512,512]{2,1,0:T(8,128)(2,1)S(1)} fusion(bf16[4,512,512]{2,1,0:T(8,128)(2,1)} %param.16, f32[4,512]{1,0:T(4,128)S(1)} %copy-done.6), kind=kLoop, calls=%fused_computation | loop fusion | flops 3145728 | bytes 4202496 | tf_op jit(solution)/shard_map/convert_element_type | solution.py:542
  32.9 11.7 %all-to-all-done.1.got_ref = bf16[16,136,128]{2,1,0:T(8,128)(2,1)S(1)} async-done(((bf16[16,136,128]{2,1,0:T(8,128)(2,1)}), bf16[16,136,128]{2,1,0:T(8,128)(2,1)S(1)}, u32[]{:S(2)}, u32[]{:S(2)}) %all-to-all-start.1) | async-done | bytes 557088 | tf_op jit(solution)/shard_map/all_to_all | solution.py:533
  45.7 1.3 %shard_map.95 = (bf16[6,32,512]{2,1,0:T(8,128)(2,1)S(1)}, bf16[10,32,512]{2,1,0:T(8,128)(2,1)S(1)}, bf16[16,8,512]{2,1,0:T(8,128)(2,1)S(1)}, bf16[6,8,512]{2,1,0:T(8,128)(2,1)S(1)}) custom-call(f32[512,256]{1,0:T(8,128)S(1)} %shard_map.94.near_ref, bf16[512,256]{1,0:T(8,128)(2,1)} %collective-permute-done.far_ref, bf16[256,512]{1,0:T(8,128)(2,1)S(1)} %copy-done.3, ...), custom_call_target="tpu_custom_call" | custom-call | flops 1150000000 | tf_op jit(solution)/shard_map/pallas_call | solution.py:392
  47.1 2.0 %collective-permute-start.3 = (bf16[6,8,512]{2,1,0:T(8,128)(2,1)S(1)}, bf16[6,8,512]{2,1,0:T(8,128)(2,1)S(1)}, u32[]{:S(2)}, u32[]{:S(2)}) collective-permute-start(bf16[6,8,512]{2,1,0:T(8,128)(2,1)S(1)} %get-tuple-element.44), channel_id=1, source_target_pairs={{0,9},{1,10},{2,11},{3,12},{4,13},{5,14},{6,15},{7,8},{8,17},{9,18... | collective-permute-start | bytes 147464 | tf_op jit(solution)/shard_map/ppermute | solution.py:470
  49.2 4.1 %collective-permute-done.1.lon_in = bf16[16,8,512]{2,1,0:T(8,128)(2,1)S(1)} collective-permute-done((bf16[16,8,512]{2,1,0:T(8,128)(2,1)S(1)}, bf16[16,8,512]{2,1,0:T(8,128)(2,1)S(1)}, u32[]{:S(2)}, u32[]{:S(2)}) %collective-permute-start.1) | collective-permute-done | bytes 131104 | tf_op jit(solution)/shard_map/ppermute | solution.py:468
  53.2 3.2 %shard_map.96 = (bf16[13,32,512]{2,1,0:T(8,128)(2,1)S(1)}, bf16[13,8,512]{2,1,0:T(8,128)(2,1)S(1)}, bf16[4,8,6,16,128]{4,3,2,1,0:T(8,128)(2,1)S(1)}) custom-call(bf16[6,32,512]{2,1,0:T(8,128)(2,1)S(1)} %get-tuple-element.39.edge_in, bf16[10,32,512]{2,1,0:T(8,128)(2,1)S(1)} %get-tuple-element.40.inner_in, ...), custom_call_target="tpu_custom_call" | custom-call | flops 1064960000 | tf_op jit(solution)/shard_map/pallas_call | solution.py:392
  56.5 2.0 %shard_map.97 = (bf16[6,32,512]{2,1,0:T(8,128)(2,1)S(1)}, bf16[19,8,512]{2,1,0:T(8,128)(2,1)S(1)}, bf16[6,8,512]{2,1,0:T(8,128)(2,1)S(1)}) custom-call(bf16[10,32,512]{2,1,0:T(8,128)(2,1)S(1)} %get-tuple-element.40.inner_in, bf16[16,8,512]{2,1,0:T(8,128)(2,1)S(1)} %collective-permute-done.1.lon_in, bf16[6,32,512]{2,1,0:T(8,128)(2,1)S(1)} %collective-permute-done.2.lat_in, ...), custom_call_target="tpu_custom_call" | custom-call | flops 491520000 | tf_op jit(solution)/shard_map/pallas_call | solution.py:392
  58.5 1.3 %collective-permute-start.4 = (bf16[19,8,512]{2,1,0:T(8,128)(2,1)S(1)}, bf16[19,8,512]{2,1,0:T(8,128)(2,1)S(1)}, u32[]{:S(2)}, u32[]{:S(2)}) collective-permute-start(bf16[19,8,512]{2,1,0:T(8,128)(2,1)S(1)} %get-tuple-element.47), channel_id=1, source_target_pairs={{1,0},{2,1},{3,2},{4,3},{5,4},{6,5},{7,6},{0,7},{9,8},{10,9},{11,1... | collective-permute-start | bytes 466952 | tf_op jit(solution)/shard_map/ppermute | solution.py:468
  62.5 3.3 %shard_map.98 = (bf16[10,32,512]{2,1,0:T(8,128)(2,1)S(1)}, bf16[10,8,512]{2,1,0:T(8,128)(2,1)S(1)}, bf16[4,8,6,16,128]{4,3,2,1,0:T(8,128)(2,1)S(1)}) custom-call(bf16[6,32,512]{2,1,0:T(8,128)(2,1)S(1)} %get-tuple-element.48.edge_in, bf16[13,32,512]{2,1,0:T(8,128)(2,1)S(1)} %get-tuple-element.43.inner_new.inner_in, ...), custom_call_target="tpu_custom_call" | custom-call | flops 819200000 | tf_op jit(solution)/shard_map/pallas_call | solution.py:392
  66.9 2.0 %shard_map.99 = (bf16[6,32,512]{2,1,0:T(8,128)(2,1)S(1)}, bf16[16,8,512]{2,1,0:T(8,128)(2,1)S(1)}, bf16[6,8,512]{2,1,0:T(8,128)(2,1)S(1)}) custom-call(bf16[13,32,512]{2,1,0:T(8,128)(2,1)S(1)} %get-tuple-element.43.inner_new.inner_in, bf16[19,8,512]{2,1,0:T(8,128)(2,1)S(1)} %collective-permute-done.4.lon_in, ...), custom_call_target="tpu_custom_call" | custom-call | flops 491520000 | tf_op jit(solution)/shard_map/pallas_call | solution.py:392
  68.9 1.2 %collective-permute-start.8 = (bf16[6,32,512]{2,1,0:T(8,128)(2,1)S(1)}, bf16[6,32,512]{2,1,0:T(8,128)(2,1)S(1)}, u32[]{:S(2)}, u32[]{:S(2)}) collective-permute-start(bf16[6,32,512]{2,1,0:T(8,128)(2,1)S(1)} %get-tuple-element.53.edge_in), channel_id=1, source_target_pairs={{0,8},{8,16},{16,24},{24,0},{1,9},{9,17},{17,25},{25,1},{2,10},{10... | collective-permute-start | bytes 589832 | tf_op jit(solution)/shard_map/ppermute | solution.py:469
  70.1 5.0 %collective-permute-done.7.lon_in = bf16[16,8,512]{2,1,0:T(8,128)(2,1)S(1)} collective-permute-done((bf16[16,8,512]{2,1,0:T(8,128)(2,1)S(1)}, bf16[16,8,512]{2,1,0:T(8,128)(2,1)S(1)}, u32[]{:S(2)}, u32[]{:S(2)}) %collective-permute-start.7) | collective-permute-done | bytes 131104 | tf_op jit(solution)/shard_map/ppermute | solution.py:468
  75.1 3.2 %shard_map.100 = (bf16[13,32,512]{2,1,0:T(8,128)(2,1)S(1)}, bf16[13,8,512]{2,1,0:T(8,128)(2,1)S(1)}, bf16[4,8,6,16,128]{4,3,2,1,0:T(8,128)(2,1)S(1)}) custom-call(bf16[6,32,512]{2,1,0:T(8,128)(2,1)S(1)} %get-tuple-element.53.edge_in, bf16[10,32,512]{2,1,0:T(8,128)(2,1)S(1)} %get-tuple-element.51.inner_new.inner_in, ...), custom_call_target="tpu_custom_call" | custom-call | flops 1064960000 | tf_op jit(solution)/shard_map/pallas_call | solution.py:392
  78.4 2.0 %shard_map.101 = (bf16[6,32,512]{2,1,0:T(8,128)(2,1)S(1)}, bf16[19,8,512]{2,1,0:T(8,128)(2,1)S(1)}, bf16[6,8,512]{2,1,0:T(8,128)(2,1)S(1)}) custom-call(bf16[10,32,512]{2,1,0:T(8,128)(2,1)S(1)} %get-tuple-element.51.inner_new.inner_in, bf16[16,8,512]{2,1,0:T(8,128)(2,1)S(1)} %collective-permute-done.7.lon_in, ...), custom_call_target="tpu_custom_call" | custom-call | flops 491520000 | tf_op jit(solution)/shard_map/pallas_call | solution.py:392
  80.4 2.7 %collective-permute-start.10 = (bf16[19,8,512]{2,1,0:T(8,128)(2,1)S(1)}, bf16[19,8,512]{2,1,0:T(8,128)(2,1)S(1)}, u32[]{:S(2)}, u32[]{:S(2)}) collective-permute-start(bf16[19,8,512]{2,1,0:T(8,128)(2,1)S(1)} %get-tuple-element.59), channel_id=1, source_target_pairs={{1,0},{2,1},{3,2},{4,3},{5,4},{6,5},{7,6},{0,7},{9,8},{10,9},{11,1... | collective-permute-start | bytes 466952 | tf_op jit(solution)/shard_map/ppermute | solution.py:468
  84.6 1.2 %collective-permute-done.10.lon_in = bf16[19,8,512]{2,1,0:T(8,128)(2,1)S(1)} collective-permute-done((bf16[19,8,512]{2,1,0:T(8,128)(2,1)S(1)}, bf16[19,8,512]{2,1,0:T(8,128)(2,1)S(1)}, u32[]{:S(2)}, u32[]{:S(2)}) %collective-permute-start.10) | collective-permute-done | bytes 155680 | tf_op jit(solution)/shard_map/ppermute | solution.py:468
  85.8 3.3 %shard_map.102 = (bf16[10,32,512]{2,1,0:T(8,128)(2,1)S(1)}, bf16[10,8,512]{2,1,0:T(8,128)(2,1)S(1)}, bf16[4,8,6,16,128]{4,3,2,1,0:T(8,128)(2,1)S(1)}) custom-call(bf16[6,32,512]{2,1,0:T(8,128)(2,1)S(1)} %get-tuple-element.60.edge_in, bf16[13,32,512]{2,1,0:T(8,128)(2,1)S(1)} %get-tuple-element.55.inner_new.inner_in, ...), custom_call_target="tpu_custom_call" | custom-call | flops 819200000 | tf_op jit(solution)/shard_map/pallas_call | solution.py:392
  89.9 2.8 %shard_map.103 = bf16[16,32,512]{2,1,0:T(8,128)(2,1)} custom-call(bf16[13,32,512]{2,1,0:T(8,128)(2,1)S(1)} %get-tuple-element.55.inner_new.inner_in, bf16[19,8,512]{2,1,0:T(8,128)(2,1)S(1)} %collective-permute-done.10.lon_in, bf16[6,32,512]{2,1,0:T(8,128)(2,1)S(1)} %collective-permute-done.11.lat_in, ...), custom_call_target="tpu_custom_call" | custom-call | flops 491520000 | tf_op jit(solution)/shard_map/pallas_call | solution.py:392
  (33 shorter events, 7.3 us)
Async XLA Ops:
  20.7 1.8 %copy-start.1 = (bf16[1024,256]{1,0:T(8,128)(2,1)S(1)}, bf16[1024,256]{1,0:T(8,128)(2,1)}, u32[]{:S(2)}) copy-start(bf16[1024,256]{1,0:T(8,128)(2,1)} %obs_ref.1) | copy-start | bytes 1572868
  20.7 1.8 %copy-start.4 = (bf16[8,1024]{1,0:T(8,128)(2,1)S(1)}, bf16[8,1024]{1,0:T(8,128)(2,1)}, u32[]{:S(2)}) copy-start(bf16[8,1024]{1,0:T(8,128)(2,1)} %get-tuple-element.36.meta_ref) | copy-start | bytes 49156
  20.7 1.8 %copy-start.5 = (s32[2,1024]{1,0:T(2,128)S(1)}, s32[2,1024]{1,0:T(2,128)}, u32[]{:S(2)}) copy-start(s32[2,1024]{1,0:T(2,128)} %get-tuple-element.35.order_ref) | copy-start | bytes 24580
  22.4 8.4 %copy-start.6 = (f32[4,512]{1,0:T(4,128)S(1)}, f32[4,512]{1,0:T(4,128)}, u32[]{:S(2)}) copy-start(f32[4,512]{1,0:T(4,128)} %param.17) | copy-start | bytes 24580
  24.5 20.1 %all-to-all-start.1 = ((bf16[16,136,128]{2,1,0:T(8,128)(2,1)}), bf16[16,136,128]{2,1,0:T(8,128)(2,1)S(1)}, u32[]{:S(2)}, u32[]{:S(2)}) async-start(bf16[16,136,128]{2,1,0:T(8,128)(2,1)} %shard_map.93), calls=%async_computation.1 | async-start | bytes 1114112 | tf_op jit(solution)/shard_map/all_to_all | solution.py:533
  28.1 17.5 %collective-permute-start = (bf16[512,256]{1,0:T(8,128)(2,1)}, bf16[512,256]{1,0:T(8,128)(2,1)}, u32[]{:S(2)}, u32[]{:S(2)}) collective-permute-start(bf16[512,256]{1,0:T(8,128)(2,1)} %shard_map.92.after_ref), channel_id=1, source_target_pairs={{0,4},{1,5},{2,6},{3,7},{4,0},{5,1},{6,2},{7,3},{8,12},{9,13},{10,... | collective-permute-start | bytes 786440 | tf_op jit(solution)/shard_map/ppermute | solution.py:525
  32.8 12.8 %copy-start.2 = (bf16[16,32,512]{2,1,0:T(8,128)(2,1)S(1)}, bf16[16,32,512]{2,1,0:T(8,128)(2,1)}, u32[]{:S(2)}) copy-start(bf16[16,32,512]{2,1,0:T(8,128)(2,1)} %back_ref.1) | copy-start | bytes 1572868
  32.9 12.8 %copy-start.3 = (bf16[256,512]{1,0:T(8,128)(2,1)S(1)}, bf16[256,512]{1,0:T(8,128)(2,1)}, u32[]{:S(2)}) copy-start(bf16[256,512]{1,0:T(8,128)(2,1)} %proj_ref.1) | copy-start | bytes 786436
  45.6 7.6 %copy-start = (f32[4,7,7,512]{3,0,2,1:T(4,128)S(1)}, f32[4,7,7,512]{3,0,2,1:T(4,128)}, u32[]{:S(2)}) copy-start(f32[4,7,7,512]{3,0,2,1:T(4,128)} %param.15) | copy-start | bytes 1204228
  47.0 6.2 %collective-permute-start.1 = (bf16[16,8,512]{2,1,0:T(8,128)(2,1)S(1)}, bf16[16,8,512]{2,1,0:T(8,128)(2,1)S(1)}, u32[]{:S(2)}, u32[]{:S(2)}) collective-permute-start(bf16[16,8,512]{2,1,0:T(8,128)(2,1)S(1)} %get-tuple-element.41), channel_id=1, source_target_pairs={{0,1},{1,2},{2,3},{3,4},{4,5},{5,6},{6,7},{7,0},{8,9},{9,10},{10,1... | collective-permute-start | bytes 393224 | tf_op jit(solution)/shard_map/ppermute | solution.py:468
  47.0 9.4 %collective-permute-start.2 = (bf16[6,32,512]{2,1,0:T(8,128)(2,1)S(1)}, bf16[6,32,512]{2,1,0:T(8,128)(2,1)S(1)}, u32[]{:S(2)}, u32[]{:S(2)}) collective-permute-start(bf16[6,32,512]{2,1,0:T(8,128)(2,1)S(1)} %get-tuple-element.39.edge_in), channel_id=1, source_target_pairs={{0,8},{8,16},{16,24},{24,0},{1,9},{9,17},{17,25},{25,1},{2,10},{10... | collective-permute-start | bytes 589832 | tf_op jit(solution)/shard_map/ppermute | solution.py:469
  47.1 9.4 %collective-permute-start.3 = (bf16[6,8,512]{2,1,0:T(8,128)(2,1)S(1)}, bf16[6,8,512]{2,1,0:T(8,128)(2,1)S(1)}, u32[]{:S(2)}, u32[]{:S(2)}) collective-permute-start(bf16[6,8,512]{2,1,0:T(8,128)(2,1)S(1)} %get-tuple-element.44), channel_id=1, source_target_pairs={{0,9},{1,10},{2,11},{3,12},{4,13},{5,14},{6,15},{7,8},{8,17},{9,18... | collective-permute-start | bytes 147464 | tf_op jit(solution)/shard_map/ppermute | solution.py:470
  58.5 4.0 %collective-permute-start.4 = (bf16[19,8,512]{2,1,0:T(8,128)(2,1)S(1)}, bf16[19,8,512]{2,1,0:T(8,128)(2,1)S(1)}, u32[]{:S(2)}, u32[]{:S(2)}) collective-permute-start(bf16[19,8,512]{2,1,0:T(8,128)(2,1)S(1)} %get-tuple-element.47), channel_id=1, source_target_pairs={{1,0},{2,1},{3,2},{4,3},{5,4},{6,5},{7,6},{0,7},{9,8},{10,9},{11,1... | collective-permute-start | bytes 466952 | tf_op jit(solution)/shard_map/ppermute | solution.py:468
  59.8 7.1 %collective-permute-start.5 = (bf16[6,32,512]{2,1,0:T(8,128)(2,1)S(1)}, bf16[6,32,512]{2,1,0:T(8,128)(2,1)S(1)}, u32[]{:S(2)}, u32[]{:S(2)}) collective-permute-start(bf16[6,32,512]{2,1,0:T(8,128)(2,1)S(1)} %get-tuple-element.48.edge_in), channel_id=1, source_target_pairs={{8,0},{16,8},{24,16},{0,24},{9,1},{17,9},{25,17},{1,25},{10,2},{18... | collective-permute-start | bytes 589832 | tf_op jit(solution)/shard_map/ppermute | solution.py:469
  60.8 5.0 %collective-permute-start.6 = (bf16[6,8,512]{2,1,0:T(8,128)(2,1)S(1)}, bf16[6,8,512]{2,1,0:T(8,128)(2,1)S(1)}, u32[]{:S(2)}, u32[]{:S(2)}) collective-permute-start(bf16[6,8,512]{2,1,0:T(8,128)(2,1)S(1)} %get-tuple-element.49), channel_id=1, source_target_pairs={{9,0},{10,1},{11,2},{12,3},{13,4},{14,5},{15,6},{8,7},{17,8},{18,9... | collective-permute-start | bytes 147464 | tf_op jit(solution)/shard_map/ppermute | solution.py:470
  68.9 6.2 %collective-permute-start.7 = (bf16[16,8,512]{2,1,0:T(8,128)(2,1)S(1)}, bf16[16,8,512]{2,1,0:T(8,128)(2,1)S(1)}, u32[]{:S(2)}, u32[]{:S(2)}) collective-permute-start(bf16[16,8,512]{2,1,0:T(8,128)(2,1)S(1)} %get-tuple-element.54), channel_id=1, source_target_pairs={{0,1},{1,2},{2,3},{3,4},{4,5},{5,6},{6,7},{7,0},{8,9},{9,10},{10,1... | collective-permute-start | bytes 393224 | tf_op jit(solution)/shard_map/ppermute | solution.py:468
  68.9 9.4 %collective-permute-start.8 = (bf16[6,32,512]{2,1,0:T(8,128)(2,1)S(1)}, bf16[6,32,512]{2,1,0:T(8,128)(2,1)S(1)}, u32[]{:S(2)}, u32[]{:S(2)}) collective-permute-start(bf16[6,32,512]{2,1,0:T(8,128)(2,1)S(1)} %get-tuple-element.53.edge_in), channel_id=1, source_target_pairs={{0,8},{8,16},{16,24},{24,0},{1,9},{9,17},{17,25},{25,1},{2,10},{10... | collective-permute-start | bytes 589832 | tf_op jit(solution)/shard_map/ppermute | solution.py:469
  70.1 8.3 %collective-permute-start.9 = (bf16[6,8,512]{2,1,0:T(8,128)(2,1)S(1)}, bf16[6,8,512]{2,1,0:T(8,128)(2,1)S(1)}, u32[]{:S(2)}, u32[]{:S(2)}) collective-permute-start(bf16[6,8,512]{2,1,0:T(8,128)(2,1)S(1)} %get-tuple-element.56), channel_id=1, source_target_pairs={{0,9},{1,10},{2,11},{3,12},{4,13},{5,14},{6,15},{7,8},{8,17},{9,18... | collective-permute-start | bytes 147464 | tf_op jit(solution)/shard_map/ppermute | solution.py:470
  80.4 5.5 %collective-permute-start.10 = (bf16[19,8,512]{2,1,0:T(8,128)(2,1)S(1)}, bf16[19,8,512]{2,1,0:T(8,128)(2,1)S(1)}, u32[]{:S(2)}, u32[]{:S(2)}) collective-permute-start(bf16[19,8,512]{2,1,0:T(8,128)(2,1)S(1)} %get-tuple-element.59), channel_id=1, source_target_pairs={{1,0},{2,1},{3,2},{4,3},{5,4},{6,5},{7,6},{0,7},{9,8},{10,9},{11,1... | collective-permute-start | bytes 466952 | tf_op jit(solution)/shard_map/ppermute | solution.py:468
  83.1 6.8 %collective-permute-start.11 = (bf16[6,32,512]{2,1,0:T(8,128)(2,1)S(1)}, bf16[6,32,512]{2,1,0:T(8,128)(2,1)S(1)}, u32[]{:S(2)}, u32[]{:S(2)}) collective-permute-start(bf16[6,32,512]{2,1,0:T(8,128)(2,1)S(1)} %get-tuple-element.60.edge_in), channel_id=1, source_target_pairs={{8,0},{16,8},{24,16},{0,24},{9,1},{17,9},{25,17},{1,25},{10,2},{18... | collective-permute-start | bytes 589832 | tf_op jit(solution)/shard_map/ppermute | solution.py:469
  84.1 5.0 %collective-permute-start.12 = (bf16[6,8,512]{2,1,0:T(8,128)(2,1)S(1)}, bf16[6,8,512]{2,1,0:T(8,128)(2,1)S(1)}, u32[]{:S(2)}, u32[]{:S(2)}) collective-permute-start(bf16[6,8,512]{2,1,0:T(8,128)(2,1)S(1)} %get-tuple-element.61), channel_id=1, source_target_pairs={{9,0},{10,1},{11,2},{12,3},{13,4},{14,5},{15,6},{8,7},{17,8},{18,9... | collective-permute-start | bytes 147464 | tf_op jit(solution)/shard_map/ppermute | solution.py:470
